TPU v7x, 512 devices: a whole 4x4x16 slice. The times are simulated.
512 devices in a mesh: rows: 128 (over z, y, core), panels: 4 (over x).
Axes of the slice: x: 4, y: 4, z: 16, core: 2. Of those that a mesh axis runs over, the one named last changes fastest.
Arguments:
- block_column: float32 [131072, 256], P('rows'), may hold values from -4 to 4
- l_panels: float32 [131072, 2, 4, 256], P('rows', None, 'panels'), may hold values from -6 to 6
- u_blocks: float32 [4, 512, 256], P('panels', 'rows'), may hold values from -0.15625 to 0.15625
- diag_inverses: float32 [4, 64, 64], replicated
- leaf_pick: int32 [128, 256], P('rows'), may hold values from 0 to 1023, as said below
- merge_pick: int32 [128, 256], replicated, may hold values from 0 to 511, as said below
- final_order: int32 [256], replicated, may hold values from 0 to 255, each once
Outputs:
- lower_panel: float32 [131072, 256], P(('rows', 'panels'))
- upper_block: float32 [256, 256], replicated
- pivot_rows: int32 [256], replicated
Inputs may be any that keep to these rules, and one draw needn't show every extreme that they name: `leaf_pick`: each row holds 256 different row numbers of that block's 1024 rows. `merge_pick`: each row holds 256 different positions among the 512 stacked rows of a merge; row 0 is not read; the picks are given and do not depend on the matrix.
All inputs are finite; a program needn't handle non-finite values.
Results may differ from a plain program's by a relative error of at most 0.0003.
Values sent between devices are 32-bit elements; how exact they have to be, the bound alone decides.
A program may use at most 64 MiB of HBM per device.

v0:
```python
import functools

import jax
import jax.numpy as jnp
from jax import lax
from jax.experimental import pallas as pl
from jax.experimental.pallas import tpu as pltpu
from jax.sharding import PartitionSpec as P

MESH = pl.DeviceIdType.MESH
F32, BF16, I32 = jnp.float32, jnp.bfloat16, jnp.int32
NZ, NY, NC, NX = 16, 4, 2, 4
FAR_FIRST = (8, 7, 9, 6, 10, 5, 11, 4, 12, 3, 13, 2, 14, 1, 15)
CLOSE = (3, 13, 2, 14, 1, 15)
NEAR = (4, 12) + CLOSE
RANGES = {"low": (0, 4), "high": (13, 16), "up": (4, 7), "down": (10, 13), "far": (7, 10),
          "w_low": (0, 6), "w_high": (11, 16), "w_far": (6, 11)}


def halves(v):
    hi = v.astype(BF16)
    return hi, (v - hi.astype(F32)).astype(BF16)


def mm(a, b):
    return jnp.dot(a, b, preferred_element_type=F32)


def mm3(a, b):
    ah, al = halves(a)
    bh, bl = halves(b)
    return mm(jnp.concatenate([ah, al], axis=1), jnp.concatenate([bh, bh], axis=0)) + mm(ah, bl)


def kernel(
    l_hbm, bc_hbm, u_hbm, leaf_hbm, mp_hbm, fo_hbm,
    xs, rows_ref, first_ref,
    l_raw, aux_raw, own, leaf, mp, fo, u_raw, rv, rs,
    xhi, xlo, g, give, keep, rc, ry, b2, sz, rz, uhi, ulo, prod, xr, xb, w, ids,
    in_sem, known, uz_s, uz_r, ub_s, ub_r, uy_s, uy_r, uc_s, uc_r,
    pc_s, pc_r, py_s, py_r, pz_s, pz_r, x_s, x_r, wz_s, wz_r, wy_s, wy_r, wc_s, wc_r, rx_s, rx_r,
    iz_s, iz_r, iy_s, iy_r, ic_s, ic_r,
):
    row = lax.axis_index("rows")
    x = lax.axis_index("panels")
    z, y, c = row // (NY * NC), (row // NC) % NY, row % NC
    rows_dev = bc_hbm.shape[0]
    quarter = rows_dev // NX

    def dev(zz, yy, cc, xx):
        return ((zz * NY + yy) * NC + cc, xx)

    def zp(k):
        return (z + k) % NZ

    def yp(k):
        return (y + k) % NY

    def xp(k):
        return (x + k) % NX

    to_z = [dev(zp(k), y, c, x) for k in range(NZ)]
    to_y = [dev(z, yp(k), c, x) for k in range(NY)]
    to_x = [dev(z, y, c, xp(k)) for k in range(NX)]
    to_c = dev(z, y, 1 - c, x)

    col = pl.multiple_of((x // 2) * 128, 128)
    mine = pl.multiple_of(x * quarter, quarter)
    loads = [
        pltpu.make_async_copy(mp_hbm.at[:, pl.ds(0, 128)], mp.at[0], in_sem.at[0]),
        pltpu.make_async_copy(fo_hbm, fo, in_sem.at[1]),
        pltpu.make_async_copy(leaf_hbm, leaf, in_sem.at[2]),
        pltpu.make_async_copy(u_hbm, u_raw, in_sem.at[3]),
        pltpu.make_async_copy(mp_hbm.at[:, pl.ds(128, 128)], mp.at[1], in_sem.at[7]),
        pltpu.make_async_copy(l_hbm, l_raw.at[pl.ds(0, 4 * rows_dev), :], in_sem.at[4]),
        pltpu.make_async_copy(bc_hbm.at[:, pl.ds(col, 128)], aux_raw.at[pl.ds(0, rows_dev), :], in_sem.at[5]),
        pltpu.make_async_copy(bc_hbm.at[pl.ds(mine, quarter), :], own, in_sem.at[6]),
    ]
    for copy in loads:
        copy.start()

    l_raw[4 * rows_dev :, :] = jnp.zeros((8, 128), F32)
    aux_raw[rows_dev:, :] = jnp.zeros((8, 128), F32)

    barrier = pltpu.get_barrier_semaphore()
    partners = [to_z[k] for k in CLOSE] + to_y[1:] + to_x[1:] + [to_c]
    for partner in partners:
        pl.semaphore_signal(barrier, inc=1, device_id=partner, device_id_type=MESH)

    sends = []
    arrivals = {}

    def send(name, src, dst, send_sem, recv_sem, to, lands):
        copy = pltpu.make_async_remote_copy(src, dst, send_sem, recv_sem, device_id=to, device_id_type=MESH)
        copy.start()
        sends.append(copy)
        came = pltpu.make_async_remote_copy(lands, lands, send_sem, recv_sem, device_id=to, device_id_type=MESH)
        arrivals.setdefault(name, []).append(came)

    def arrive(*names):
        for name in names:
            for copy in arrivals.pop(name)[::-1]:
                copy.wait_recv()

    def settle(count):
        for copy in sends[:count]:
            copy.wait_send()
        del sends[:count]

    for copy in loads[3:4]:
        copy.wait()
    for i in range(4):
        for h in range(2):
            g[0, y, c, 2 * i + h : 2 * i + h + 1, :] = u_raw[i : i + 1, 128 * h : 128 * h + 128]

    for copy in loads[:3] + loads[4:5]:
        copy.wait()
    down = lax.broadcasted_iota(I32, (8, 128), 0)

    def picked(half0, half1, at):
        low = at & 127
        return jnp.where(at >= 128, jnp.take_along_axis(half1, low, axis=1), jnp.take_along_axis(half0, low, axis=1))

    def looked_up(table, first, stride, count, owner, at):
        if count < 8:
            total = jnp.zeros((8, 128), F32)
            for i in range(count):
                line = first + i * stride
                rows = [jnp.broadcast_to(table[h, line : line + 1, :], (8, 128)) for h in range(2)]
                total = jnp.where(owner == i, picked(*rows, at).astype(F32), total)
            return total
        total = jnp.zeros((8, 128), F32)
        for i in range(0, count, 8):
            rows = [table[h, pl.ds(first + i * stride, 8, stride=stride), :] for h in range(2)]
            total += jnp.where(owner - i == down, picked(*rows, at).astype(F32), 0.0)
        return jnp.broadcast_to(jnp.sum(total, axis=0, keepdims=True), (8, 128))

    for s in range(2):
        at = jnp.broadcast_to(fo[:, 128 * s : 128 * s + 128], (8, 128))
        block = jnp.zeros((8, 128), I32)
        for level in reversed(range(7)):
            found = looked_up(mp, 1 << level, 2 << level, 64 >> level, block, at).astype(I32)
            block = 2 * block + (found >> 8)
            at = found & 255
        rows = [jnp.broadcast_to(leaf[:, 128 * h : 128 * h + 128], (8, 128)) for h in range(2)]
        first_ref[:, 128 * s : 128 * s + 128] = rows_dev * block[0:1]
        rv[:, 128 * s : 128 * s + 128] = jnp.where(block == row, picked(*rows, at), rows_dev)[0:1]
    to_scalars = pltpu.make_async_copy(rv, rs, in_sem.at[8])
    to_scalars.start()

    pl.semaphore_wait(barrier, len(partners))
    for k in CLOSE:
        at = NZ - k
        send(("uz", at), g.at[0, y, c], g.at[at, y, c], uz_s.at[k], uz_r.at[k], to_z[k], g.at[at, y, c])

    to_scalars.wait()
    for copy in loads[5:]:
        copy.wait()

    quarter_lane = lax.broadcasted_iota(I32, (rows_dev, 128), 1) // 64 == x % 2
    numbers = lax.broadcasted_iota(I32, (rows_dev, 128), 0).astype(F32)
    aux_raw[:rows_dev, :] = jnp.where(quarter_lane, aux_raw[:rows_dev, :], numbers)

    def gather(into, core, k):
        base = core * 128 + yp(k) * 32
        for i in range(32):
            at = rs[0, base + i]
            for j in range(4):
                into[i : i + 1, 128 * j : 128 * j + 128] = l_raw[pl.ds(4 * at + j, 1), :]
            into[i : i + 1, 512:640] = aux_raw[pl.ds(at, 1), :]

    def hand_over(k):
        gather(give.at[k], 1 - c, k)
        send(("pc", k), give.at[k], rc.at[k], pc_s.at[k], pc_r.at[k], to_c, rc.at[k])

    def fold(k):
        gather(keep.at[k], c, k)
        arrive(("pc", k))
        keep[k] = keep[k] + rc[k]
        send("py", keep.at[k], ry.at[k], py_s.at[k], py_r.at[k], to_y[k], ry.at[k])

    hand_over(2)
    hand_over(1)
    fold(2)
    hand_over(3)
    fold(1)
    hand_over(0)
    fold(3)
    gather(keep.at[0], c, 0)
    arrive(("pc", 0))

    def on_in_y(name, buf, s_sem, r_sem, which, at):
        first, last = RANGES[which]
        part = pl.ds(first, last - first)
        for k in (2, 1, 3):
            send((name, which), buf.at[part, y, c], buf.at[part, y, c], s_sem.at[at, k], r_sem.at[at, k],
                 to_y[k], buf.at[part, yp(NY - k), c])

    def on_to_core(name, buf, s_sem, r_sem, which, at):
        first, last = RANGES[which]
        part = pl.ds(first, last - first)
        send((name, which), buf.at[part, :, c], buf.at[part, :, c], s_sem.at[at], r_sem.at[at], to_c,
             buf.at[part, :, 1 - c])

    def second(name, at, k, first, last, there):
        src, dst = pl.ds(first, last - first), pl.ds(there, last - first)
        send(name, g.at[src, y, c], g.at[dst, y, c], ub_s.at[at], ub_r.at[at], to_z[k], g.at[dst, y, c])

    arrive(*[("uz", at) for at in (1, 15, 2, 14, 3, 13)])
    second("far up", 0, 11, 2, 4, 7)
    second("far down", 1, 5, 14, 15, 9)
    second("up", 2, 13, 1, 4, 4)
    second("down", 3, 3, 13, 16, 10)
    for k in (3, 13):
        pl.semaphore_signal(known, inc=1, device_id=to_z[k], device_id_type=MESH)
    on_in_y("uy", g, uy_s, uy_r, "low", 0)
    on_in_y("uy", g, uy_s, uy_r, "high", 1)

    for part in range(NX):
        rows = pl.ds(part * quarter, quarter)
        for j in range(4):
            hi, lo = halves(l_raw[pl.ds(part * quarter * 4 + j, quarter, stride=4), :])
            xhi[rows, 128 * j : 128 * j + 128] = hi
            xlo[rows, 128 * j : 128 * j + 128] = lo

    arrive("py")
    b2[...] = keep[0] + rc[0] + ry[1] + ry[2] + ry[3]
    for zz in range(NZ):
        for j in range(5):
            sz[zz, j] = b2[2 * zz : 2 * zz + 2, 128 * j : 128 * j + 128]
    pl.semaphore_wait(known, 2)
    for k in FAR_FIRST:
        send("pz", sz.at[zp(k)], rz.at[k], pz_s.at[k], pz_r.at[k], to_z[k], rz.at[k])
    arrive("up")
    on_in_y("uy", g, uy_s, uy_r, "up", 2)
    arrive("down")
    on_in_y("uy", g, uy_s, uy_r, "down", 3)
    arrive("far up", "far down")
    on_in_y("uy", g, uy_s, uy_r, "far", 4)
    settle(17)
    arrive(("uy", "low"))
    on_to_core("uc", g, uc_s, uc_r, "low", 0)
    arrive(("uy", "high"))
    on_to_core("uc", g, uc_s, uc_r, "high", 1)
    flat = g.reshape(NZ * NY * NC * 8, 128)

    def rounded(k):
        rows = pl.ds(pl.multiple_of(zp(k) * 32, 32), 32)
        for h in range(2):
            hi, lo = halves(flat[pl.ds(k * 64 + h, 32, stride=2), :])
            uhi[rows, 128 * h : 128 * h + 128] = hi
            ulo[rows, 128 * h : 128 * h + 128] = lo

    arrive(("uc", "low"), ("uc", "high"))
    for k in (0, 1, 2, 3, 13, 14, 15):
        rounded(k)
    arrive(("uy", "up"))
    on_to_core("uc", g, uc_s, uc_r, "up", 2)
    arrive(("uy", "down"))
    on_to_core("uc", g, uc_s, uc_r, "down", 3)
    arrive(("uy", "far"))
    on_to_core("uc", g, uc_s, uc_r, "far", 4)
    arrive(("uc", "up"), ("uc", "down"))
    for k in (4, 5, 6, 10, 11, 12):
        rounded(k)
    arrive(("uc", "far"))
    for k in (7, 8, 9):
        rounded(k)

    mine2 = sz[z]
    arrive("pz")
    for k in range(1, NZ):
        mine2 = mine2 + rz[k]
    two = jnp.concatenate([mine2[j] for j in range(4)], axis=1)
    two_hi = two.astype(BF16).astype(F32)
    stacked = jnp.concatenate([two_hi, two - two_hi, jnp.zeros((12, 512), F32)], axis=0).astype(BF16)
    by_hi = mm(stacked, uhi[...])
    by_lo = mm(stacked, ulo[...])
    two = by_hi[0:2] + (by_hi[2:4] + by_lo[0:2])
    for h in range(2):
        carried = jnp.where(quarter_lane[:2], jnp.where(x // 2 == h, mine2[4], 0.0), 0.0)
        xb[x, 2 * h : 2 * h + 2, :] = carried - two[:, 128 * h : 128 * h + 128]
    for k in (2, 1, 3):
        send("x", xb.at[x], xb.at[x], x_s.at[k], x_r.at[k], to_x[k], xb.at[xp(NX - k)])

    half = quarter // 2

    def partial(k):
        for h in range(2):
            rows = pl.ds(pl.multiple_of(xp(k) * quarter + h * half, half), half)
            left, right = xhi[rows, :], uhi[...]
            prod[k, h] = mm(left, right) + (mm(xlo[rows, :], right) + mm(left, ulo[...]))

    def to_neighbour(name, k, src, at):
        send((name, k), src, xr.at[at], rx_s.at[at], rx_r.at[at], to_x[k], xr.at[at])

    partial(2)
    to_neighbour("relay", 1, prod.at[2, 0], 0)
    to_neighbour("relay", 3, prod.at[2, 1], 1)

    number = jnp.max(jnp.where(quarter_lane[:2], 0.0, mine2[4]), axis=1, keepdims=True)
    left = lax.broadcasted_iota(I32, (1, 128), 1) < 64
    ids[0, y, c] = jnp.where(left, number[0:1], number[1:2])
    for k in FAR_FIRST:
        at = NZ - k
        send("iz", ids.at[0, y, c], ids.at[at, y, c], iz_s.at[k], iz_r.at[k], to_z[k], ids.at[at, y, c])

    arrive("x")
    w[0, y, c] = xb[0] + xb[1] + xb[2] + xb[3]
    def far(k):
        for j in (2, 1, 3, 0):
            send(("wf", j), w.at[0, y, c], w.at[NZ - k, y, c], wz_s.at[k, j], wz_r.at[k, j],
                 dev(zp(k), yp(j), c, x), w.at[NZ - k, yp(NY - j), c])

    def near(k):
        at = NZ - k
        send(("wz", at), w.at[0, y, c], w.at[at, y, c], wz_s.at[k, 0], wz_r.at[k, 0], to_z[k], w.at[at, y, c])

    for step, k in ((far, 8), (far, 7), (far, 9), (near, 5), (near, 11), (far, 6), (far, 10)):
        step(k)
    for k in NEAR:
        near(k)

    partial(1)
    to_neighbour("rx", 1, prod.at[1, 1], 2)
    partial(3)
    to_neighbour("rx", 3, prod.at[3, 0], 3)
    partial(0)

    arrive(*[("wz", at) for at in (1, 2, 3, 4, 5)])
    on_in_y("wy", w, wy_s, wy_r, "w_low", 0)
    arrive(*[("wz", at) for at in (15, 14, 13, 12, 11)])
    on_in_y("wy", w, wy_s, wy_r, "w_high", 1)
    arrive("iz")
    for k in (2, 1, 3):
        send("iy", ids.at[:, y, c], ids.at[:, y, c], iy_s.at[k], iy_r.at[k], to_y[k], ids.at[:, yp(NY - k), c])
    arrive(("relay", 1))
    prod[1, 0] = prod[1, 0] + xr[0]
    to_neighbour("rx2", 1, prod.at[1, 0], 4)
    arrive(("relay", 3))
    prod[3, 1] = prod[3, 1] + xr[1]
    to_neighbour("rx2", 3, prod.at[3, 1], 5)
    arrive(("wy", "w_low"))
    on_to_core("wc", w, wc_s, wc_r, "w_low", 0)
    arrive(("wy", "w_high"))
    on_to_core("wc", w, wc_s, wc_r, "w_high", 1)
    settle(len(sends) - 12)
    arrive(("wf", 0), ("wf", 1), ("wf", 3), ("wf", 2))
    on_to_core("wc", w, wc_s, wc_r, "w_far", 2)
    arrive("iy")
    send("ic", ids.at[:, :, c], ids.at[:, :, c], ic_s.at[0], ic_r.at[0], to_c, ids.at[:, :, 1 - c])
    arrive(("rx", 1), ("rx", 3), ("rx2", 1), ("rx2", 3))
    xs[256 : 256 + half, :] = own[:half, :] - (prod[0, 0] + xr[3] + xr[4])
    xs[256 + half :, :] = own[half:, :] - (prod[0, 1] + xr[2] + xr[5])
    arrive("ic")
    for slot in range(NC * NY * NZ):
        cc, yy, zz = slot // (NY * NZ), slot // NZ % NY, slot % NZ
        rows_ref[slot : slot + 1, :] = ids[(zz - z + NZ) % NZ, yy, cc]

    settle(len(sends) - 4)
    arrive(("wc", "w_low"), ("wc", "w_high"), ("wc", "w_far"))
    for slot in range(NC * NY * NZ):
        cc, yy, zz = slot // (NY * NZ), slot // NZ % NY, slot % NZ
        for h in range(2):
            piece = w[(zz - z + NZ) % NZ, yy, cc, 2 * h : 2 * h + 2, :]
            xs[2 * slot : 2 * slot + 2, 128 * h : 128 * h + 128] = piece

    settle(len(sends))


def factor(xs, dinv, rows_in, first_in, low_ref, up_ref, piv_ref):
    number = rows_in[...].T
    lane = lax.broadcasted_iota(I32, (8, 128), 1)
    for s in range(2):
        even, odd = (
            jnp.take_along_axis(jnp.broadcast_to(number[i : i + 1], (8, 128)), 64 * s + lane // 2, axis=1) for i in (0, 64)
        )
        found = jnp.where(lane % 2 == 0, even, odd)[0:1].astype(I32)
        piv_ref[:, 128 * s : 128 * s + 128] = first_in[:, 128 * s : 128 * s + 128] + found
    right = lax.broadcasted_iota(I32, (64, 128), 1) >= 64
    pivots = [xs[:256, 128 * h : 128 * h + 128] for h in range(2)]
    rest = [xs[256:, 128 * h : 128 * h + 128] for h in range(2)]
    for t in range(4):
        inverse = dinv[t]
        at, first = t // 2, 64 * (t % 2)
        u_t = [v[:64] for v in pivots]
        for h in range(2):
            if h < at:
                shown = jnp.zeros((64, 128), F32)
            else:
                shown = jnp.where(right, u_t[h], 0.0) if h == at and first else u_t[h]
            up_ref[64 * t : 64 * t + 64, 128 * h : 128 * h + 128] = shown
        panel = rest[at][:, first : first + 64]
        low_ref[:, 64 * t : 64 * t + 64] = mm3(panel, inverse)
        if t < 3:
            above = pivots[at][64:, first : first + 64]
            pivots = [v[64:] for v in pivots]
            for h in range(at + (first > 0), 2):
                step = mm3(inverse, jnp.where(right, u_t[h], 0.0) if h == at else u_t[h])
                pivots[h] = pivots[h] - mm3(above, step)
                rest[h] = rest[h] - mm3(panel, step)


def in_hbm(array):
    return pltpu.with_memory_space_constraint(array, pltpu.HBM)


def body(block_column, l_panels, u_blocks, diag_inverses, leaf_pick, merge_pick, final_order):
    rows_dev, cols = block_column.shape
    quarter = rows_dev // NX
    vmem = pl.BlockSpec(memory_space=pltpu.VMEM)
    sem = pltpu.SemaphoreType.DMA
    xs, numbers, first = pl.pallas_call(
        kernel,
        name="panel",
        out_shape=(
            jax.ShapeDtypeStruct((256 + quarter, cols), F32),
            jax.ShapeDtypeStruct((128, 128), F32),
            jax.ShapeDtypeStruct((1, cols), I32),
        ),
        in_specs=[pl.BlockSpec(memory_space=pltpu.HBM)] * 6,
        out_specs=(vmem,) * 3,
        scratch_shapes=[
            pltpu.VMEM((rows_dev * 4 + 8, 128), F32),
            pltpu.VMEM((rows_dev + 8, 128), F32),
            pltpu.VMEM((quarter, cols), F32),
            pltpu.VMEM((1, 256), I32),
            pltpu.VMEM((2, 128, 128), I32),
            pltpu.VMEM((1, 256), I32),
            pltpu.VMEM((4, 256), F32),
            pltpu.VMEM((1, 256), I32),
            pltpu.SMEM((1, 256), I32),
            pltpu.VMEM((rows_dev, 512), BF16),
            pltpu.VMEM((rows_dev, 512), BF16),
            pltpu.VMEM((NZ, NY, NC, 8, 128), F32),
            pltpu.VMEM((NY, 32, 640), F32),
            pltpu.VMEM((NY, 32, 640), F32),
            pltpu.VMEM((NY, 32, 640), F32),
            pltpu.VMEM((NY, 32, 640), F32),
            pltpu.VMEM((32, 640), F32),
            pltpu.VMEM((NZ, 5, 2, 128), F32),
            pltpu.VMEM((NZ, 5, 2, 128), F32),
            pltpu.VMEM((512, cols), BF16),
            pltpu.VMEM((512, cols), BF16),
            pltpu.VMEM((NX, 2, quarter // 2, cols), F32),
            pltpu.VMEM((6, quarter // 2, cols), F32),
            pltpu.VMEM((NX, 4, 128), F32),
            pltpu.VMEM((NZ, NY, NC, 4, 128), F32),
            pltpu.VMEM((NZ, NY, NC, 1, 128), F32),
            sem((9,)),
            pltpu.SemaphoreType.REGULAR,
            sem((NZ,)), sem((NZ,)), sem((4,)), sem((4,)), sem((5, NY)), sem((5, NY)), sem((5,)), sem((5,)),
            sem((NY,)), sem((NY,)), sem((NY,)), sem((NY,)), sem((NZ,)), sem((NZ,)),
            sem((NX,)), sem((NX,)),
            sem((NZ, NY)), sem((NZ, NY)), sem((4, NY)), sem((4, NY)), sem((4,)), sem((4,)),
            sem((6,)), sem((6,)),
            sem((NZ,)), sem((NZ,)), sem((NY,)), sem((NY,)), sem((1,)), sem((1,)),
        ],
        compiler_params=pltpu.CompilerParams(
            collective_id=0, has_side_effects=True, vmem_limit_bytes=24 * 1024 * 1024
        ),
    )(
        in_hbm(l_panels.reshape(-1, 128)),
        in_hbm(block_column),
        in_hbm(u_blocks[0]),
        in_hbm(leaf_pick),
        in_hbm(merge_pick),
        in_hbm(final_order.reshape(1, -1)),
    )
    low, up, piv = pl.pallas_call(
        factor,
        name="factor",
        out_shape=(
            jax.ShapeDtypeStruct((quarter, cols), F32),
            jax.ShapeDtypeStruct((cols, cols), F32),
            jax.ShapeDtypeStruct((1, cols), I32),
        ),
        in_specs=[vmem] * 4,
        out_specs=(vmem,) * 3,
        compiler_params=pltpu.CompilerParams(vmem_limit_bytes=8 * 1024 * 1024),
    )(xs, diag_inverses, numbers, first)
    return low, up, piv[0]


def solution(mesh):
    return jax.shard_map(
        body,
        mesh=mesh,
        in_specs=(
            P("rows", None),
            P("rows", None, "panels", None),
            P("panels", "rows", None),
            P(),
            P("rows", None),
            P(),
            P(),
        ),
        out_specs=(P(("rows", "panels"), None), P(), P()),
        check_vma=False,
    )
```

profile of v0, /device:TPU:1, one launch (start us, length us, event | category | flops | bytes accessed | tf_op | source)
XLA Modules:
  0.0 51.0 jit_solution(12030458143730106648)
XLA Ops:
  0.6 0.0 copy-start
  0.6 48.1 %panel.1 = (f32[512,256]{1,0:T(8,128)S(1)}, f32[128,128]{1,0:T(8,128)S(1)}, s32[1,256]{1,0:T(1,128)S(1)}) custom-call(f32[4096,128]{1,0:T(8,128)} %bitcast.4, f32[1024,256]{1,0:T(8,128)} %bc_hbm.1, f32[4,256]{1,0:T(4,128)} %bitcast.5, s32[1,256]{1,0:T(1,128)} %leaf_hbm.1, s32[128,256]{1,0:T(8,128)} %mp_hbm.1, s32[1,256]{1,0:T(1,128)} %bitcast.6), custom_call_target="tpu_custom_call" | custom-call | tf_op jit(solution)/shard_map/panel/pallas_call | solution.py:413
  48.8 0.0 copy-done
  48.8 2.3 %factor.1 = (f32[256,256]{1,0:T(8,128)}, f32[256,256]{1,0:T(8,128)}, s32[1,256]{1,0:T(1,128)}) custom-call(f32[512,256]{1,0:T(8,128)S(1)} %get-tuple-element.9.xs, f32[4,64,64]{2,1,0:T(8,128)S(1)} %copy-done, f32[128,128]{1,0:T(8,128)S(1)} %get-tuple-element.10.rows_in, s32[1,256]{1,0:T(1,128)S(1)} %get-tuple-element.11.first_in), custom_call_target="tpu_custom_call" | custom-call | tf_op jit(solution)/shard_map/factor/pallas_call | solution.py:470
Async XLA Ops:
  0.6 48.1 %copy-start = (f32[4,64,64]{2,1,0:T(8,128)S(1)}, f32[4,64,64]{2,1,0:T(8,128)}, u32[]{:S(2)}) copy-start(f32[4,64,64]{2,1,0:T(8,128)} %dinv.1) | copy-start | bytes 196612
where the time goes:
time: 51.2 us; the launch traced here: 51 us
  Pallas kernels  50.4 us (98%)
  between operations  0.66 us (1%)
    pallas_call x1, Pallas kernels, body(): pl.pallas_call(kernel, name='panel', out_shape=(jax.ShapeDtypeStruct((256...  48.1 us
    pallas_call x1, Pallas kernels, body(): pl.pallas_call(factor, name='factor', out_shape=(jax.ShapeDtypeStruct((qu...  2.26 us

commit v1 on v0

--- a/solution.py
+++ b/solution.py
@@ -17,6 +17,14 @@
           "w_low": (0, 6), "w_high": (11, 16), "w_far": (6, 11)}
 
 
+SENT = ("uz", "ub", "uy", "uc", "pc", "py", "pz", "x", "wz", "wy", "wc", "rx", "iz", "iy", "ic")
+LANDED = (
+    "uz", "ub", "ub far", "uy", "uy mid", "uy far", "uc", "uc mid", "uc far", "pc0", "pc1", "pc2", "pc3", "py", "pz", "x",
+    "wz low", "wz high", "wz far", "wy low", "wy high", "wc low", "wc high", "wc far", "relay1", "relay3", "rx",
+    "iz", "iy", "ic",
+)
+
+
 def halves(v):
     hi = v.astype(BF16)
     return hi, (v - hi.astype(F32)).astype(BF16)
@@ -37,9 +45,7 @@
     xs, rows_ref, first_ref,
     l_raw, aux_raw, own, leaf, mp, fo, u_raw, rv, rs,
     xhi, xlo, g, give, keep, rc, ry, b2, sz, rz, uhi, ulo, prod, xr, xb, w, ids,
-    in_sem, known, uz_s, uz_r, ub_s, ub_r, uy_s, uy_r, uc_s, uc_r,
-    pc_s, pc_r, py_s, py_r, pz_s, pz_r, x_s, x_r, wz_s, wz_r, wy_s, wy_r, wc_s, wc_r, rx_s, rx_r,
-    iz_s, iz_r, iy_s, iy_r, ic_s, ic_r,
+    in_sem, known, send_sem, recv_sem,
 ):
     row = lax.axis_index("rows")
     x = lax.axis_index("panels")
@@ -76,36 +82,30 @@
         pltpu.make_async_copy(bc_hbm.at[:, pl.ds(col, 128)], aux_raw.at[pl.ds(0, rows_dev), :], in_sem.at[5]),
         pltpu.make_async_copy(bc_hbm.at[pl.ds(mine, quarter), :], own, in_sem.at[6]),
     ]
-    for copy in loads:
-        copy.start()
-
-    l_raw[4 * rows_dev :, :] = jnp.zeros((8, 128), F32)
-    aux_raw[rows_dev:, :] = jnp.zeros((8, 128), F32)
-
     barrier = pltpu.get_barrier_semaphore()
     partners = [to_z[k] for k in CLOSE] + to_y[1:] + to_x[1:] + [to_c]
     for partner in partners:
         pl.semaphore_signal(barrier, inc=1, device_id=partner, device_id_type=MESH)
 
-    sends = []
-    arrivals = {}
-
-    def send(name, src, dst, send_sem, recv_sem, to, lands):
-        copy = pltpu.make_async_remote_copy(src, dst, send_sem, recv_sem, device_id=to, device_id_type=MESH)
+    for copy in loads:
         copy.start()
-        sends.append(copy)
-        came = pltpu.make_async_remote_copy(lands, lands, send_sem, recv_sem, device_id=to, device_id_type=MESH)
-        arrivals.setdefault(name, []).append(came)
-
-    def arrive(*names):
-        for name in names:
-            for copy in arrivals.pop(name)[::-1]:
-                copy.wait_recv()
-
-    def settle(count):
-        for copy in sends[:count]:
-            copy.wait_send()
-        del sends[:count]
+
+    l_raw[4 * rows_dev :, :] = jnp.zeros((8, 128), F32)
+    aux_raw[rows_dev:, :] = jnp.zeros((8, 128), F32)
+
+    def copy_to(to, src, dst, out, into):
+        return pltpu.make_async_remote_copy(
+            src, dst, send_sem.at[SENT.index(out)], recv_sem.at[LANDED.index(into)], device_id=to, device_id_type=MESH
+        )
+
+    def send(to, src, dst, out, into):
+        copy_to(to, src, dst, out, into).start()
+
+    def arrive(into, whole):
+        copy_to(to_c, whole, whole, SENT[0], into).wait_recv()
+
+    def sent(out, whole):
+        copy_to(to_c, whole, whole, out, LANDED[0]).wait_send()
 
     for copy in loads[3:4]:
         copy.wait()
@@ -151,7 +151,7 @@
     pl.semaphore_wait(barrier, len(partners))
     for k in CLOSE:
         at = NZ - k
-        send(("uz", at), g.at[0, y, c], g.at[at, y, c], uz_s.at[k], uz_r.at[k], to_z[k], g.at[at, y, c])
+        send(to_z[k], g.at[0, y, c], g.at[at, y, c], "uz", "uz")
 
     to_scalars.wait()
     for copy in loads[5:]:
@@ -171,13 +171,13 @@
 
     def hand_over(k):
         gather(give.at[k], 1 - c, k)
-        send(("pc", k), give.at[k], rc.at[k], pc_s.at[k], pc_r.at[k], to_c, rc.at[k])
+        send(to_c, give.at[k], rc.at[k], "pc", f"pc{k}")
 
     def fold(k):
         gather(keep.at[k], c, k)
-        arrive(("pc", k))
+        arrive(f"pc{k}", rc.at[k])
         keep[k] = keep[k] + rc[k]
-        send("py", keep.at[k], ry.at[k], py_s.at[k], py_r.at[k], to_y[k], ry.at[k])
+        send(to_y[k], keep.at[k], ry.at[k], "py", "py")
 
     hand_over(2)
     hand_over(1)
@@ -187,34 +187,30 @@
     hand_over(0)
     fold(3)
     gather(keep.at[0], c, 0)
-    arrive(("pc", 0))
-
-    def on_in_y(name, buf, s_sem, r_sem, which, at):
+    arrive("pc0", rc.at[0])
+
+    def on_in_y(buf, which, out, into):
         first, last = RANGES[which]
         part = pl.ds(first, last - first)
         for k in (2, 1, 3):
-            send((name, which), buf.at[part, y, c], buf.at[part, y, c], s_sem.at[at, k], r_sem.at[at, k],
-                 to_y[k], buf.at[part, yp(NY - k), c])
-
-    def on_to_core(name, buf, s_sem, r_sem, which, at):
+            send(to_y[k], buf.at[part, y, c], buf.at[part, y, c], out, into)
+
+    def on_to_core(buf, which, out, into):
         first, last = RANGES[which]
         part = pl.ds(first, last - first)
-        send((name, which), buf.at[part, :, c], buf.at[part, :, c], s_sem.at[at], r_sem.at[at], to_c,
-             buf.at[part, :, 1 - c])
-
-    def second(name, at, k, first, last, there):
+        send(to_c, buf.at[part, :, c], buf.at[part, :, c], out, into)
+
+    def second(into, k, first, last, there):
         src, dst = pl.ds(first, last - first), pl.ds(there, last - first)
-        send(name, g.at[src, y, c], g.at[dst, y, c], ub_s.at[at], ub_r.at[at], to_z[k], g.at[dst, y, c])
-
-    arrive(*[("uz", at) for at in (1, 15, 2, 14, 3, 13)])
-    second("far up", 0, 11, 2, 4, 7)
-    second("far down", 1, 5, 14, 15, 9)
-    second("up", 2, 13, 1, 4, 4)
-    second("down", 3, 3, 13, 16, 10)
+        send(to_z[k], g.at[src, y, c], g.at[dst, y, c], "ub", into)
+
+    arrive("uz", g.at[pl.ds(0, 6), y, c])
+    second("ub far", 11, 2, 4, 7)
+    second("ub far", 5, 14, 15, 9)
+    second("ub", 13, 1, 4, 4)
+    second("ub", 3, 13, 16, 10)
     for k in (3, 13):
         pl.semaphore_signal(known, inc=1, device_id=to_z[k], device_id_type=MESH)
-    on_in_y("uy", g, uy_s, uy_r, "low", 0)
-    on_in_y("uy", g, uy_s, uy_r, "high", 1)
 
     for part in range(NX):
         rows = pl.ds(part * quarter, quarter)
@@ -223,25 +219,24 @@
             xhi[rows, 128 * j : 128 * j + 128] = hi
             xlo[rows, 128 * j : 128 * j + 128] = lo
 
-    arrive("py")
+    arrive("py", ry.at[pl.ds(1, 3)])
     b2[...] = keep[0] + rc[0] + ry[1] + ry[2] + ry[3]
     for zz in range(NZ):
         for j in range(5):
             sz[zz, j] = b2[2 * zz : 2 * zz + 2, 128 * j : 128 * j + 128]
     pl.semaphore_wait(known, 2)
     for k in FAR_FIRST:
-        send("pz", sz.at[zp(k)], rz.at[k], pz_s.at[k], pz_r.at[k], to_z[k], rz.at[k])
-    arrive("up")
-    on_in_y("uy", g, uy_s, uy_r, "up", 2)
-    arrive("down")
-    on_in_y("uy", g, uy_s, uy_r, "down", 3)
-    arrive("far up", "far down")
-    on_in_y("uy", g, uy_s, uy_r, "far", 4)
-    settle(17)
-    arrive(("uy", "low"))
-    on_to_core("uc", g, uc_s, uc_r, "low", 0)
-    arrive(("uy", "high"))
-    on_to_core("uc", g, uc_s, uc_r, "high", 1)
+        send(to_z[k], sz.at[zp(k)], rz.at[k], "pz", "pz")
+    on_in_y(g, "low", "uy", "uy")
+    on_in_y(g, "high", "uy", "uy")
+    arrive("ub", g.at[pl.ds(0, 6), y, c])
+    on_in_y(g, "up", "uy", "uy mid")
+    on_in_y(g, "down", "uy", "uy mid")
+    arrive("ub far", g.at[pl.ds(0, 3), y, c])
+    on_in_y(g, "far", "uy", "uy far")
+    arrive("uy", g.at[pl.ds(0, 7), pl.ds(0, 3), c])
+    on_to_core(g, "low", "uc", "uc")
+    on_to_core(g, "high", "uc", "uc")
     flat = g.reshape(NZ * NY * NC * 8, 128)
 
     def rounded(k):
@@ -251,24 +246,23 @@
             uhi[rows, 128 * h : 128 * h + 128] = hi
             ulo[rows, 128 * h : 128 * h + 128] = lo
 
-    arrive(("uc", "low"), ("uc", "high"))
+    arrive("uc", g.at[pl.ds(0, 7), :, c])
     for k in (0, 1, 2, 3, 13, 14, 15):
         rounded(k)
-    arrive(("uy", "up"))
-    on_to_core("uc", g, uc_s, uc_r, "up", 2)
-    arrive(("uy", "down"))
-    on_to_core("uc", g, uc_s, uc_r, "down", 3)
-    arrive(("uy", "far"))
-    on_to_core("uc", g, uc_s, uc_r, "far", 4)
-    arrive(("uc", "up"), ("uc", "down"))
+    arrive("uy mid", g.at[pl.ds(0, 6), pl.ds(0, 3), c])
+    on_to_core(g, "up", "uc", "uc mid")
+    on_to_core(g, "down", "uc", "uc mid")
+    arrive("uy far", g.at[pl.ds(0, 3), pl.ds(0, 3), c])
+    on_to_core(g, "far", "uc", "uc far")
+    arrive("uc mid", g.at[pl.ds(0, 6), :, c])
     for k in (4, 5, 6, 10, 11, 12):
         rounded(k)
-    arrive(("uc", "far"))
+    arrive("uc far", g.at[pl.ds(0, 3), :, c])
     for k in (7, 8, 9):
         rounded(k)
 
     mine2 = sz[z]
-    arrive("pz")
+    arrive("pz", rz.at[pl.ds(1, NZ - 1)])
     for k in range(1, NZ):
         mine2 = mine2 + rz[k]
     two = jnp.concatenate([mine2[j] for j in range(4)], axis=1)
@@ -281,7 +275,7 @@
         carried = jnp.where(quarter_lane[:2], jnp.where(x // 2 == h, mine2[4], 0.0), 0.0)
         xb[x, 2 * h : 2 * h + 2, :] = carried - two[:, 128 * h : 128 * h + 128]
     for k in (2, 1, 3):
-        send("x", xb.at[x], xb.at[x], x_s.at[k], x_r.at[k], to_x[k], xb.at[xp(NX - k)])
+        send(to_x[k], xb.at[x], xb.at[x], "x", "x")
 
     half = quarter // 2
 
@@ -291,30 +285,28 @@
             left, right = xhi[rows, :], uhi[...]
             prod[k, h] = mm(left, right) + (mm(xlo[rows, :], right) + mm(left, ulo[...]))
 
-    def to_neighbour(name, k, src, at):
-        send((name, k), src, xr.at[at], rx_s.at[at], rx_r.at[at], to_x[k], xr.at[at])
+    def to_neighbour(into, k, src, at):
+        send(to_x[k], src, xr.at[at], "rx", into)
 
     partial(2)
-    to_neighbour("relay", 1, prod.at[2, 0], 0)
-    to_neighbour("relay", 3, prod.at[2, 1], 1)
+    to_neighbour("relay1", 1, prod.at[2, 0], 0)
+    to_neighbour("relay3", 3, prod.at[2, 1], 1)
 
     number = jnp.max(jnp.where(quarter_lane[:2], 0.0, mine2[4]), axis=1, keepdims=True)
     left = lax.broadcasted_iota(I32, (1, 128), 1) < 64
     ids[0, y, c] = jnp.where(left, number[0:1], number[1:2])
     for k in FAR_FIRST:
         at = NZ - k
-        send("iz", ids.at[0, y, c], ids.at[at, y, c], iz_s.at[k], iz_r.at[k], to_z[k], ids.at[at, y, c])
-
-    arrive("x")
+        send(to_z[k], ids.at[0, y, c], ids.at[at, y, c], "iz", "iz")
+
+    arrive("x", xb.at[pl.ds(0, 3)])
     w[0, y, c] = xb[0] + xb[1] + xb[2] + xb[3]
     def far(k):
         for j in (2, 1, 3, 0):
-            send(("wf", j), w.at[0, y, c], w.at[NZ - k, y, c], wz_s.at[k, j], wz_r.at[k, j],
-                 dev(zp(k), yp(j), c, x), w.at[NZ - k, yp(NY - j), c])
+            send(dev(zp(k), yp(j), c, x), w.at[0, y, c], w.at[NZ - k, y, c], "wz", "wz far")
 
     def near(k):
-        at = NZ - k
-        send(("wz", at), w.at[0, y, c], w.at[at, y, c], wz_s.at[k, 0], wz_r.at[k, 0], to_z[k], w.at[at, y, c])
+        send(to_z[k], w.at[0, y, c], w.at[NZ - k, y, c], "wz", "wz low" if NZ - k < 8 else "wz high")
 
     for step, k in ((far, 8), (far, 7), (far, 9), (near, 5), (near, 11), (far, 6), (far, 10)):
         step(k)
@@ -327,45 +319,59 @@
     to_neighbour("rx", 3, prod.at[3, 0], 3)
     partial(0)
 
-    arrive(*[("wz", at) for at in (1, 2, 3, 4, 5)])
-    on_in_y("wy", w, wy_s, wy_r, "w_low", 0)
-    arrive(*[("wz", at) for at in (15, 14, 13, 12, 11)])
-    on_in_y("wy", w, wy_s, wy_r, "w_high", 1)
-    arrive("iz")
+    arrive("wz low", w.at[pl.ds(0, 5), y, c])
+    on_in_y(w, "w_low", "wy", "wy low")
+    arrive("wz high", w.at[pl.ds(0, 5), y, c])
+    on_in_y(w, "w_high", "wy", "wy high")
+    arrive("iz", ids.at[pl.ds(1, NZ - 1), y, c])
     for k in (2, 1, 3):
-        send("iy", ids.at[:, y, c], ids.at[:, y, c], iy_s.at[k], iy_r.at[k], to_y[k], ids.at[:, yp(NY - k), c])
-    arrive(("relay", 1))
+        send(to_y[k], ids.at[:, y, c], ids.at[:, y, c], "iy", "iy")
+    arrive("relay1", xr.at[0])
     prod[1, 0] = prod[1, 0] + xr[0]
-    to_neighbour("rx2", 1, prod.at[1, 0], 4)
-    arrive(("relay", 3))
+    to_neighbour("rx", 1, prod.at[1, 0], 4)
+    arrive("relay3", xr.at[1])
     prod[3, 1] = prod[3, 1] + xr[1]
-    to_neighbour("rx2", 3, prod.at[3, 1], 5)
-    arrive(("wy", "w_low"))
-    on_to_core("wc", w, wc_s, wc_r, "w_low", 0)
-    arrive(("wy", "w_high"))
-    on_to_core("wc", w, wc_s, wc_r, "w_high", 1)
-    settle(len(sends) - 12)
-    arrive(("wf", 0), ("wf", 1), ("wf", 3), ("wf", 2))
-    on_to_core("wc", w, wc_s, wc_r, "w_far", 2)
-    arrive("iy")
-    send("ic", ids.at[:, :, c], ids.at[:, :, c], ic_s.at[0], ic_r.at[0], to_c, ids.at[:, :, 1 - c])
-    arrive(("rx", 1), ("rx", 3), ("rx2", 1), ("rx2", 3))
+    to_neighbour("rx", 3, prod.at[3, 1], 5)
+    arrive("wy low", w.at[pl.ds(0, 6), pl.ds(0, 3), c])
+    on_to_core(w, "w_low", "wc", "wc low")
+    arrive("wy high", w.at[pl.ds(0, 5), pl.ds(0, 3), c])
+    on_to_core(w, "w_high", "wc", "wc high")
+    sent("uz", g.at[pl.ds(0, 6), y, c])
+    sent("ub", g.at[pl.ds(0, 9), y, c])
+    sent("uy", g.at[:, pl.ds(0, 3), c])
+    sent("uc", g.at[:, :, c])
+    sent("pc", give)
+    sent("py", keep.at[pl.ds(0, 3)])
+    sent("pz", sz.at[pl.ds(0, NZ - 1)])
+    sent("x", xb.at[pl.ds(0, 3)])
+    sent("iz", ids.at[pl.ds(0, NZ - 1), y, c])
+    arrive("wz far", w.at[pl.ds(0, 5), :, c])
+    on_to_core(w, "w_far", "wc", "wc far")
+    arrive("iy", ids.at[:, pl.ds(0, 3), c])
+    send(to_c, ids.at[:, :, c], ids.at[:, :, c], "ic", "ic")
+    arrive("rx", xr.at[pl.ds(2, 4)])
     xs[256 : 256 + half, :] = own[:half, :] - (prod[0, 0] + xr[3] + xr[4])
     xs[256 + half :, :] = own[half:, :] - (prod[0, 1] + xr[2] + xr[5])
-    arrive("ic")
+    arrive("ic", ids.at[:, :, 1 - c])
     for slot in range(NC * NY * NZ):
         cc, yy, zz = slot // (NY * NZ), slot // NZ % NY, slot % NZ
         rows_ref[slot : slot + 1, :] = ids[(zz - z + NZ) % NZ, yy, cc]
 
-    settle(len(sends) - 4)
-    arrive(("wc", "w_low"), ("wc", "w_high"), ("wc", "w_far"))
+    sent("wz", w.at[pl.ds(0, 15), pl.ds(0, 2), c])
+    sent("wy", w.at[pl.ds(0, 11), pl.ds(0, 3), c])
+    sent("rx", xr)
+    sent("iy", ids.at[:, pl.ds(0, 3), c])
+    arrive("wc low", w.at[pl.ds(0, 6), :, c])
+    arrive("wc high", w.at[pl.ds(0, 5), :, c])
+    arrive("wc far", w.at[pl.ds(0, 5), :, c])
     for slot in range(NC * NY * NZ):
         cc, yy, zz = slot // (NY * NZ), slot // NZ % NY, slot % NZ
         for h in range(2):
             piece = w[(zz - z + NZ) % NZ, yy, cc, 2 * h : 2 * h + 2, :]
             xs[2 * slot : 2 * slot + 2, 128 * h : 128 * h + 128] = piece
 
-    settle(len(sends))
+    sent("wc", w.at[:, :, c])
+    sent("ic", ids.at[:, :, c])
 
 
 def factor(xs, dinv, rows_in, first_in, low_ref, up_ref, piv_ref):
@@ -449,12 +455,8 @@
             pltpu.VMEM((NZ, NY, NC, 1, 128), F32),
             sem((9,)),
             pltpu.SemaphoreType.REGULAR,
-            sem((NZ,)), sem((NZ,)), sem((4,)), sem((4,)), sem((5, NY)), sem((5, NY)), sem((5,)), sem((5,)),
-            sem((NY,)), sem((NY,)), sem((NY,)), sem((NY,)), sem((NZ,)), sem((NZ,)),
-            sem((NX,)), sem((NX,)),
-            sem((NZ, NY)), sem((NZ, NY)), sem((4, NY)), sem((4, NY)), sem((4,)), sem((4,)),
-            sem((6,)), sem((6,)),
-            sem((NZ,)), sem((NZ,)), sem((NY,)), sem((NY,)), sem((1,)), sem((1,)),
+            sem((len(SENT),)),
+            sem((len(LANDED),)),
         ],
         compiler_params=pltpu.CompilerParams(
             collective_id=0, has_side_effects=True, vmem_limit_bytes=24 * 1024 * 1024

time: 51.2 us -> 49 us (0.957)
  Pallas kernels: 50.4 us -> 48.2 us
    pallas_call x1, Pallas kernels: 48.1 us -> 46 us  [body(): pl.pallas_call(kernel, name='panel', out_shape=(jax.ShapeDtypeStruct((256...]
where the time goes in v1:
time: 49 us; the launch traced here: 48.9 us
  Pallas kernels  48.2 us (98%)
  between operations  0.66 us (1%)
    pallas_call x1, Pallas kernels, body(): pl.pallas_call(kernel, name='panel', out_shape=(jax.ShapeDtypeStruct((256...  46 us
    pallas_call x1, Pallas kernels, body(): pl.pallas_call(factor, name='factor', out_shape=(jax.ShapeDtypeStruct((qu...  2.26 us

profile of v1, /device:TPU:1, one launch (start us, length us, event | category | flops | bytes accessed | tf_op | source)
XLA Modules:
  0.0 48.9 jit_solution(9455097959757208795)
XLA Ops:
  0.6 0.0 copy-start
  0.6 46.0 %panel.1 = (f32[512,256]{1,0:T(8,128)S(1)}, f32[128,128]{1,0:T(8,128)S(1)}, s32[1,256]{1,0:T(1,128)S(1)}) custom-call(f32[4096,128]{1,0:T(8,128)} %bitcast.4, f32[1024,256]{1,0:T(8,128)} %bc_hbm.1, f32[4,256]{1,0:T(4,128)} %bitcast.5, s32[1,256]{1,0:T(1,128)} %leaf_hbm.1, s32[128,256]{1,0:T(8,128)} %mp_hbm.1, s32[1,256]{1,0:T(1,128)} %bitcast.6), custom_call_target="tpu_custom_call" | custom-call | tf_op jit(solution)/shard_map/panel/pallas_call | solution.py:419
  46.6 0.0 copy-done
  46.6 2.3 %factor.1 = (f32[256,256]{1,0:T(8,128)}, f32[256,256]{1,0:T(8,128)}, s32[1,256]{1,0:T(1,128)}) custom-call(f32[512,256]{1,0:T(8,128)S(1)} %get-tuple-element.9.xs, f32[4,64,64]{2,1,0:T(8,128)S(1)} %copy-done, f32[128,128]{1,0:T(8,128)S(1)} %get-tuple-element.10.rows_in, s32[1,256]{1,0:T(1,128)S(1)} %get-tuple-element.11.first_in), custom_call_target="tpu_custom_call" | custom-call | tf_op jit(solution)/shard_map/factor/pallas_call | solution.py:472
Async XLA Ops:
  0.6 46.0 %copy-start = (f32[4,64,64]{2,1,0:T(8,128)S(1)}, f32[4,64,64]{2,1,0:T(8,128)}, u32[]{:S(2)}) copy-start(f32[4,64,64]{2,1,0:T(8,128)} %dinv.1) | copy-start | bytes 196612

commit v2 on v1

--- a/solution.py
+++ b/solution.py
@@ -17,11 +17,11 @@
           "w_low": (0, 6), "w_high": (11, 16), "w_far": (6, 11)}
 
 
-SENT = ("uz", "ub", "uy", "uc", "pc", "py", "pz", "x", "wz", "wy", "wc", "rx", "iz", "iy", "ic")
+SENT = ("uz", "ub", "uy", "uc", "pc", "py", "pz", "x", "wz", "wy", "wc", "rx", "nc", "ny", "nz")
 LANDED = (
     "uz", "ub", "ub far", "uy", "uy mid", "uy far", "uc", "uc mid", "uc far", "pc0", "pc1", "pc2", "pc3", "py", "pz", "x",
     "wz low", "wz high", "wz far", "wy low", "wy high", "wc low", "wc high", "wc far", "relay1", "relay3", "rx",
-    "iz", "iy", "ic",
+    "nc", "ny", "nz",
 )
 
 
@@ -42,9 +42,9 @@
 
 def kernel(
     l_hbm, bc_hbm, u_hbm, leaf_hbm, mp_hbm, fo_hbm,
-    xs, rows_ref, first_ref,
+    xs, piv_ref,
     l_raw, aux_raw, own, leaf, mp, fo, u_raw, rv, rs,
-    xhi, xlo, g, give, keep, rc, ry, b2, sz, rz, uhi, ulo, prod, xr, xb, w, ids,
+    xhi, xlo, g, give, keep, rc, ry, b2, sz, rz, uhi, ulo, prod, xr, xb, w, nv, nc, ny, nz,
     in_sem, known, send_sem, recv_sem,
 ):
     row = lax.axis_index("rows")
@@ -143,8 +143,9 @@
             block = 2 * block + (found >> 8)
             at = found & 255
         rows = [jnp.broadcast_to(leaf[:, 128 * h : 128 * h + 128], (8, 128)) for h in range(2)]
-        first_ref[:, 128 * s : 128 * s + 128] = rows_dev * block[0:1]
-        rv[:, 128 * s : 128 * s + 128] = jnp.where(block == row, picked(*rows, at), rows_dev)[0:1]
+        line = picked(*rows, at)
+        rv[:, 128 * s : 128 * s + 128] = jnp.where(block == row, line, rows_dev)[0:1]
+        nv[:, 128 * s : 128 * s + 128] = jnp.where(block == row, rows_dev * block + line, 0)[0:1]
     to_scalars = pltpu.make_async_copy(rv, rs, in_sem.at[8])
     to_scalars.start()
 
@@ -158,16 +159,18 @@
         copy.wait()
 
     quarter_lane = lax.broadcasted_iota(I32, (rows_dev, 128), 1) // 64 == x % 2
-    numbers = lax.broadcasted_iota(I32, (rows_dev, 128), 0).astype(F32)
-    aux_raw[:rows_dev, :] = jnp.where(quarter_lane, aux_raw[:rows_dev, :], numbers)
+    wide = aux_raw[:rows_dev, :]
+    aux_raw[:rows_dev, :] = jnp.where(quarter_lane, wide, pltpu.roll(wide, 64, axis=1))
+    left = lax.broadcasted_iota(I32, (8, 128), 1) < 64
 
     def gather(into, core, k):
         base = core * 128 + yp(k) * 32
-        for i in range(32):
-            at = rs[0, base + i]
-            for j in range(4):
-                into[i : i + 1, 128 * j : 128 * j + 128] = l_raw[pl.ds(4 * at + j, 1), :]
-            into[i : i + 1, 512:640] = aux_raw[pl.ds(at, 1), :]
+        for i in range(0, 32, 2):
+            pair = rs[0, base + i], rs[0, base + i + 1]
+            for n in range(8):
+                into[4 * i + n : 4 * i + n + 1, :] = l_raw[pl.ds(4 * pair[n // 4] + n % 4, 1), :]
+            first, second = (aux_raw[pl.ds(at, 1), :] for at in pair)
+            into[128 + i // 2 : 129 + i // 2, :] = jnp.where(left[:1], first, second)
 
     def hand_over(k):
         gather(give.at[k], 1 - c, k)
@@ -179,6 +182,7 @@
         keep[k] = keep[k] + rc[k]
         send(to_y[k], keep.at[k], ry.at[k], "py", "py")
 
+    send(to_c, nv, nc, "nc", "nc")
     hand_over(2)
     hand_over(1)
     fold(2)
@@ -188,6 +192,10 @@
     fold(3)
     gather(keep.at[0], c, 0)
     arrive("pc0", rc.at[0])
+    arrive("nc", nc)
+    ny[0] = nv[...] + nc[...]
+    for k in (2, 1, 3):
+        send(to_y[k], ny.at[0], ny.at[k], "ny", "ny")
 
     def on_in_y(buf, which, out, into):
         first, last = RANGES[which]
@@ -222,8 +230,9 @@
     arrive("py", ry.at[pl.ds(1, 3)])
     b2[...] = keep[0] + rc[0] + ry[1] + ry[2] + ry[3]
     for zz in range(NZ):
-        for j in range(5):
-            sz[zz, j] = b2[2 * zz : 2 * zz + 2, 128 * j : 128 * j + 128]
+        for line in range(9):
+            at = 8 * zz + line if line < 8 else 128 + zz
+            sz[zz, line] = b2[at : at + 1, :]
     pl.semaphore_wait(known, 2)
     for k in FAR_FIRST:
         send(to_z[k], sz.at[zp(k)], rz.at[k], "pz", "pz")
@@ -265,14 +274,17 @@
     arrive("pz", rz.at[pl.ds(1, NZ - 1)])
     for k in range(1, NZ):
         mine2 = mine2 + rz[k]
-    two = jnp.concatenate([mine2[j] for j in range(4)], axis=1)
+    two = jnp.concatenate([jnp.concatenate([mine2[4 * i + j] for j in range(4)], axis=1) for i in range(2)], axis=0)
     two_hi = two.astype(BF16).astype(F32)
     stacked = jnp.concatenate([two_hi, two - two_hi, jnp.zeros((12, 512), F32)], axis=0).astype(BF16)
     by_hi = mm(stacked, uhi[...])
     by_lo = mm(stacked, ulo[...])
     two = by_hi[0:2] + (by_hi[2:4] + by_lo[0:2])
+    both = jnp.broadcast_to(mine2[8], (8, 128))
+    swapped = pltpu.roll(both, 64, axis=1)
+    both = jnp.concatenate([jnp.where(left, both, swapped)[:1], jnp.where(left, swapped, both)[:1]], axis=0)
     for h in range(2):
-        carried = jnp.where(quarter_lane[:2], jnp.where(x // 2 == h, mine2[4], 0.0), 0.0)
+        carried = jnp.where(quarter_lane[:2], jnp.where(x // 2 == h, both, 0.0), 0.0)
         xb[x, 2 * h : 2 * h + 2, :] = carried - two[:, 128 * h : 128 * h + 128]
     for k in (2, 1, 3):
         send(to_x[k], xb.at[x], xb.at[x], "x", "x")
@@ -292,12 +304,10 @@
     to_neighbour("relay1", 1, prod.at[2, 0], 0)
     to_neighbour("relay3", 3, prod.at[2, 1], 1)
 
-    number = jnp.max(jnp.where(quarter_lane[:2], 0.0, mine2[4]), axis=1, keepdims=True)
-    left = lax.broadcasted_iota(I32, (1, 128), 1) < 64
-    ids[0, y, c] = jnp.where(left, number[0:1], number[1:2])
+    arrive("ny", ny.at[pl.ds(1, 3)])
+    nz[0] = ny[0] + ny[1] + ny[2] + ny[3]
     for k in FAR_FIRST:
-        at = NZ - k
-        send(to_z[k], ids.at[0, y, c], ids.at[at, y, c], "iz", "iz")
+        send(to_z[k], nz.at[0], nz.at[k], "nz", "nz")
 
     arrive("x", xb.at[pl.ds(0, 3)])
     w[0, y, c] = xb[0] + xb[1] + xb[2] + xb[3]
@@ -323,9 +333,6 @@
     on_in_y(w, "w_low", "wy", "wy low")
     arrive("wz high", w.at[pl.ds(0, 5), y, c])
     on_in_y(w, "w_high", "wy", "wy high")
-    arrive("iz", ids.at[pl.ds(1, NZ - 1), y, c])
-    for k in (2, 1, 3):
-        send(to_y[k], ids.at[:, y, c], ids.at[:, y, c], "iy", "iy")
     arrive("relay1", xr.at[0])
     prod[1, 0] = prod[1, 0] + xr[0]
     to_neighbour("rx", 1, prod.at[1, 0], 4)
@@ -344,23 +351,22 @@
     sent("py", keep.at[pl.ds(0, 3)])
     sent("pz", sz.at[pl.ds(0, NZ - 1)])
     sent("x", xb.at[pl.ds(0, 3)])
-    sent("iz", ids.at[pl.ds(0, NZ - 1), y, c])
+    sent("nc", nv)
+    sent("ny", ny.at[pl.ds(1, 3)])
+    sent("nz", nz.at[pl.ds(1, NZ - 1)])
     arrive("wz far", w.at[pl.ds(0, 5), :, c])
     on_to_core(w, "w_far", "wc", "wc far")
-    arrive("iy", ids.at[:, pl.ds(0, 3), c])
-    send(to_c, ids.at[:, :, c], ids.at[:, :, c], "ic", "ic")
     arrive("rx", xr.at[pl.ds(2, 4)])
     xs[256 : 256 + half, :] = own[:half, :] - (prod[0, 0] + xr[3] + xr[4])
     xs[256 + half :, :] = own[half:, :] - (prod[0, 1] + xr[2] + xr[5])
-    arrive("ic", ids.at[:, :, 1 - c])
-    for slot in range(NC * NY * NZ):
-        cc, yy, zz = slot // (NY * NZ), slot // NZ % NY, slot % NZ
-        rows_ref[slot : slot + 1, :] = ids[(zz - z + NZ) % NZ, yy, cc]
-
+    arrive("nz", nz.at[pl.ds(1, NZ - 1)])
+    number = nz[0]
+    for k in range(1, NZ):
+        number = number + nz[k]
+    piv_ref[...] = number
     sent("wz", w.at[pl.ds(0, 15), pl.ds(0, 2), c])
     sent("wy", w.at[pl.ds(0, 11), pl.ds(0, 3), c])
     sent("rx", xr)
-    sent("iy", ids.at[:, pl.ds(0, 3), c])
     arrive("wc low", w.at[pl.ds(0, 6), :, c])
     arrive("wc high", w.at[pl.ds(0, 5), :, c])
     arrive("wc far", w.at[pl.ds(0, 5), :, c])
@@ -371,18 +377,10 @@
             xs[2 * slot : 2 * slot + 2, 128 * h : 128 * h + 128] = piece
 
     sent("wc", w.at[:, :, c])
-    sent("ic", ids.at[:, :, c])
-
-
-def factor(xs, dinv, rows_in, first_in, low_ref, up_ref, piv_ref):
-    number = rows_in[...].T
-    lane = lax.broadcasted_iota(I32, (8, 128), 1)
-    for s in range(2):
-        even, odd = (
-            jnp.take_along_axis(jnp.broadcast_to(number[i : i + 1], (8, 128)), 64 * s + lane // 2, axis=1) for i in (0, 64)
-        )
-        found = jnp.where(lane % 2 == 0, even, odd)[0:1].astype(I32)
-        piv_ref[:, 128 * s : 128 * s + 128] = first_in[:, 128 * s : 128 * s + 128] + found
+
+
+def factor(xs, dinv, piv_in, low_ref, up_ref, piv_ref):
+    piv_ref[...] = piv_in[...]
     right = lax.broadcasted_iota(I32, (64, 128), 1) >= 64
     pivots = [xs[:256, 128 * h : 128 * h + 128] for h in range(2)]
     rest = [xs[256:, 128 * h : 128 * h + 128] for h in range(2)]
@@ -416,16 +414,15 @@
     quarter = rows_dev // NX
     vmem = pl.BlockSpec(memory_space=pltpu.VMEM)
     sem = pltpu.SemaphoreType.DMA
-    xs, numbers, first = pl.pallas_call(
+    xs, piv = pl.pallas_call(
         kernel,
         name="panel",
         out_shape=(
             jax.ShapeDtypeStruct((256 + quarter, cols), F32),
-            jax.ShapeDtypeStruct((128, 128), F32),
             jax.ShapeDtypeStruct((1, cols), I32),
         ),
         in_specs=[pl.BlockSpec(memory_space=pltpu.HBM)] * 6,
-        out_specs=(vmem,) * 3,
+        out_specs=(vmem,) * 2,
         scratch_shapes=[
             pltpu.VMEM((rows_dev * 4 + 8, 128), F32),
             pltpu.VMEM((rows_dev + 8, 128), F32),
@@ -439,20 +436,23 @@
             pltpu.VMEM((rows_dev, 512), BF16),
             pltpu.VMEM((rows_dev, 512), BF16),
             pltpu.VMEM((NZ, NY, NC, 8, 128), F32),
-            pltpu.VMEM((NY, 32, 640), F32),
-            pltpu.VMEM((NY, 32, 640), F32),
-            pltpu.VMEM((NY, 32, 640), F32),
-            pltpu.VMEM((NY, 32, 640), F32),
-            pltpu.VMEM((32, 640), F32),
-            pltpu.VMEM((NZ, 5, 2, 128), F32),
-            pltpu.VMEM((NZ, 5, 2, 128), F32),
+            pltpu.VMEM((NY, 144, 128), F32),
+            pltpu.VMEM((NY, 144, 128), F32),
+            pltpu.VMEM((NY, 144, 128), F32),
+            pltpu.VMEM((NY, 144, 128), F32),
+            pltpu.VMEM((144, 128), F32),
+            pltpu.VMEM((NZ, 9, 1, 128), F32),
+            pltpu.VMEM((NZ, 9, 1, 128), F32),
             pltpu.VMEM((512, cols), BF16),
             pltpu.VMEM((512, cols), BF16),
             pltpu.VMEM((NX, 2, quarter // 2, cols), F32),
             pltpu.VMEM((6, quarter // 2, cols), F32),
             pltpu.VMEM((NX, 4, 128), F32),
             pltpu.VMEM((NZ, NY, NC, 4, 128), F32),
-            pltpu.VMEM((NZ, NY, NC, 1, 128), F32),
+            pltpu.VMEM((1, 256), I32),
+            pltpu.VMEM((1, 256), I32),
+            pltpu.VMEM((NY, 1, 256), I32),
+            pltpu.VMEM((NZ, 1, 256), I32),
             sem((9,)),
             pltpu.SemaphoreType.REGULAR,
             sem((len(SENT),)),
@@ -477,10 +477,10 @@
             jax.ShapeDtypeStruct((cols, cols), F32),
             jax.ShapeDtypeStruct((1, cols), I32),
         ),
-        in_specs=[vmem] * 4,
+        in_specs=[vmem] * 3,
         out_specs=(vmem,) * 3,
         compiler_params=pltpu.CompilerParams(vmem_limit_bytes=8 * 1024 * 1024),
-    )(xs, diag_inverses, numbers, first)
+    )(xs, diag_inverses, piv)
     return low, up, piv[0]
 
 

time: 49 us -> 47.3 us (0.965)
  Pallas kernels: 48.2 us -> 46.5 us
    pallas_call x1, Pallas kernels: 46 us -> 44.3 us  [body(): pl.pallas_call(kernel, name='panel', out_shape=(jax.ShapeDtypeStruct((256...]
where the time goes in v2:
time: 47.3 us; the launch traced here: 47.2 us
  Pallas kernels  46.5 us (98%)
  between operations  0.66 us (1%)
    pallas_call x1, Pallas kernels, body(): pl.pallas_call(kernel, name='panel', out_shape=(jax.ShapeDtypeStruct((256...  44.3 us
    pallas_call x1, Pallas kernels, body(): pl.pallas_call(factor, name='factor', out_shape=(jax.ShapeDtypeStruct((qu...  2.26 us

profile of v2, /device:TPU:1, one launch (start us, length us, event | category | flops | bytes accessed | tf_op | source)
XLA Modules:
  0.0 47.2 jit_solution(16643960955618649768)
XLA Ops:
  0.6 0.0 copy-start
  0.6 44.3 %panel.1 = (f32[512,256]{1,0:T(8,128)S(1)}, s32[1,256]{1,0:T(1,128)S(1)}) custom-call(f32[4096,128]{1,0:T(8,128)} %bitcast.4, f32[1024,256]{1,0:T(8,128)} %bc_hbm.1, f32[4,256]{1,0:T(4,128)} %bitcast.5, s32[1,256]{1,0:T(1,128)} %leaf_hbm.1, s32[128,256]{1,0:T(8,128)} %mp_hbm.1, s32[1,256]{1,0:T(1,128)} %bitcast.6), custom_call_target="tpu_custom_call" | custom-call | tf_op jit(solution)/shard_map/panel/pallas_call | solution.py:417
  44.9 0.0 copy-done
  45.0 2.3 %factor.1 = (f32[256,256]{1,0:T(8,128)}, f32[256,256]{1,0:T(8,128)}, s32[1,256]{1,0:T(1,128)}) custom-call(f32[512,256]{1,0:T(8,128)S(1)} %get-tuple-element.8.xs, f32[4,64,64]{2,1,0:T(8,128)S(1)} %copy-done, s32[1,256]{1,0:T(1,128)S(1)} %get-tuple-element.9.piv_in), custom_call_target="tpu_custom_call" | custom-call | tf_op jit(solution)/shard_map/factor/pallas_call | solution.py:472
Async XLA Ops:
  0.6 44.3 %copy-start = (f32[4,64,64]{2,1,0:T(8,128)S(1)}, f32[4,64,64]{2,1,0:T(8,128)}, u32[]{:S(2)}) copy-start(f32[4,64,64]{2,1,0:T(8,128)} %dinv.1) | copy-start | bytes 196612

commit v3 on v2

--- a/solution.py
+++ b/solution.py
@@ -246,6 +246,11 @@
     arrive("uy", g.at[pl.ds(0, 7), pl.ds(0, 3), c])
     on_to_core(g, "low", "uc", "uc")
     on_to_core(g, "high", "uc", "uc")
+    arrive("uy mid", g.at[pl.ds(0, 6), pl.ds(0, 3), c])
+    on_to_core(g, "up", "uc", "uc mid")
+    on_to_core(g, "down", "uc", "uc mid")
+    arrive("uy far", g.at[pl.ds(0, 3), pl.ds(0, 3), c])
+    on_to_core(g, "far", "uc", "uc far")
     flat = g.reshape(NZ * NY * NC * 8, 128)
 
     def rounded(k):
@@ -258,11 +263,6 @@
     arrive("uc", g.at[pl.ds(0, 7), :, c])
     for k in (0, 1, 2, 3, 13, 14, 15):
         rounded(k)
-    arrive("uy mid", g.at[pl.ds(0, 6), pl.ds(0, 3), c])
-    on_to_core(g, "up", "uc", "uc mid")
-    on_to_core(g, "down", "uc", "uc mid")
-    arrive("uy far", g.at[pl.ds(0, 3), pl.ds(0, 3), c])
-    on_to_core(g, "far", "uc", "uc far")
     arrive("uc mid", g.at[pl.ds(0, 6), :, c])
     for k in (4, 5, 6, 10, 11, 12):
         rounded(k)
@@ -339,10 +339,6 @@
     arrive("relay3", xr.at[1])
     prod[3, 1] = prod[3, 1] + xr[1]
     to_neighbour("rx", 3, prod.at[3, 1], 5)
-    arrive("wy low", w.at[pl.ds(0, 6), pl.ds(0, 3), c])
-    on_to_core(w, "w_low", "wc", "wc low")
-    arrive("wy high", w.at[pl.ds(0, 5), pl.ds(0, 3), c])
-    on_to_core(w, "w_high", "wc", "wc high")
     sent("uz", g.at[pl.ds(0, 6), y, c])
     sent("ub", g.at[pl.ds(0, 9), y, c])
     sent("uy", g.at[:, pl.ds(0, 3), c])
@@ -356,25 +352,33 @@
     sent("nz", nz.at[pl.ds(1, NZ - 1)])
     arrive("wz far", w.at[pl.ds(0, 5), :, c])
     on_to_core(w, "w_far", "wc", "wc far")
+    arrive("wy low", w.at[pl.ds(0, 6), pl.ds(0, 3), c])
+    on_to_core(w, "w_low", "wc", "wc low")
+    arrive("wy high", w.at[pl.ds(0, 5), pl.ds(0, 3), c])
+    on_to_core(w, "w_high", "wc", "wc high")
     arrive("rx", xr.at[pl.ds(2, 4)])
-    xs[256 : 256 + half, :] = own[:half, :] - (prod[0, 0] + xr[3] + xr[4])
-    xs[256 + half :, :] = own[half:, :] - (prod[0, 1] + xr[2] + xr[5])
+    xs[2] = own[:half, :] - (prod[0, 0] + xr[3] + xr[4])
+    xs[3] = own[half:, :] - (prod[0, 1] + xr[2] + xr[5])
     arrive("nz", nz.at[pl.ds(1, NZ - 1)])
     number = nz[0]
     for k in range(1, NZ):
         number = number + nz[k]
     piv_ref[...] = number
+
+    def place(core):
+        for slot in range(NY * NZ):
+            for h in range(2):
+                piece = w[(slot % NZ - z + NZ) % NZ, slot // NZ, core, 2 * h : 2 * h + 2, :]
+                xs[core, 2 * slot : 2 * slot + 2, 128 * h : 128 * h + 128] = piece
+
+    place(c)
     sent("wz", w.at[pl.ds(0, 15), pl.ds(0, 2), c])
     sent("wy", w.at[pl.ds(0, 11), pl.ds(0, 3), c])
     sent("rx", xr)
     arrive("wc low", w.at[pl.ds(0, 6), :, c])
     arrive("wc high", w.at[pl.ds(0, 5), :, c])
     arrive("wc far", w.at[pl.ds(0, 5), :, c])
-    for slot in range(NC * NY * NZ):
-        cc, yy, zz = slot // (NY * NZ), slot // NZ % NY, slot % NZ
-        for h in range(2):
-            piece = w[(zz - z + NZ) % NZ, yy, cc, 2 * h : 2 * h + 2, :]
-            xs[2 * slot : 2 * slot + 2, 128 * h : 128 * h + 128] = piece
+    place(1 - c)
 
     sent("wc", w.at[:, :, c])
 
@@ -382,8 +386,9 @@
 def factor(xs, dinv, piv_in, low_ref, up_ref, piv_ref):
     piv_ref[...] = piv_in[...]
     right = lax.broadcasted_iota(I32, (64, 128), 1) >= 64
-    pivots = [xs[:256, 128 * h : 128 * h + 128] for h in range(2)]
-    rest = [xs[256:, 128 * h : 128 * h + 128] for h in range(2)]
+    lanes = [slice(128 * h, 128 * h + 128) for h in range(2)]
+    pivots = [jnp.concatenate([xs[0, :, at], xs[1, :, at]], axis=0) for at in lanes]
+    rest = [jnp.concatenate([xs[2, :, at], xs[3, :, at]], axis=0) for at in lanes]
     for t in range(4):
         inverse = dinv[t]
         at, first = t // 2, 64 * (t % 2)
@@ -418,7 +423,7 @@
         kernel,
         name="panel",
         out_shape=(
-            jax.ShapeDtypeStruct((256 + quarter, cols), F32),
+            jax.ShapeDtypeStruct((4, quarter // 2, cols), F32),
             jax.ShapeDtypeStruct((1, cols), I32),
         ),
         in_specs=[pl.BlockSpec(memory_space=pltpu.HBM)] * 6,

time: 47.3 us -> 48.1 us (1.017)
  Pallas kernels: 46.5 us -> 47.3 us
    pallas_call x1, Pallas kernels: 44.3 us -> 45 us  [body(): pl.pallas_call(kernel, name='panel', out_shape=(jax.ShapeDtypeStruct((4,...]
where the time goes in v3:
time: 48.1 us; the launch traced here: 47.9 us
  Pallas kernels  47.3 us (98%)
  between operations  0.66 us (1%)
    pallas_call x1, Pallas kernels, body(): pl.pallas_call(kernel, name='panel', out_shape=(jax.ShapeDtypeStruct((4,...  45 us
    pallas_call x1, Pallas kernels, body(): pl.pallas_call(factor, name='factor', out_shape=(jax.ShapeDtypeStruct((qu...  2.26 us

profile of v3, /device:TPU:1, one launch (start us, length us, event | category | flops | bytes accessed | tf_op | source)
XLA Modules:
  0.0 47.9 jit_solution(18307602004071217116)
XLA Ops:
  0.6 0.0 copy-start
  0.6 45.0 %panel.1 = (f32[4,128,256]{2,1,0:T(8,128)S(1)}, s32[1,256]{1,0:T(1,128)S(1)}) custom-call(f32[4096,128]{1,0:T(8,128)} %bitcast.4, f32[1024,256]{1,0:T(8,128)} %bc_hbm.1, f32[4,256]{1,0:T(4,128)} %bitcast.5, s32[1,256]{1,0:T(1,128)} %leaf_hbm.1, s32[128,256]{1,0:T(8,128)} %mp_hbm.1, s32[1,256]{1,0:T(1,128)} %bitcast.6), custom_call_target="tpu_custom_call" | custom-call | tf_op jit(solution)/shard_map/panel/pallas_call | solution.py:422
  45.7 0.0 copy-done
  45.7 2.3 %factor.1 = (f32[256,256]{1,0:T(8,128)}, f32[256,256]{1,0:T(8,128)}, s32[1,256]{1,0:T(1,128)}) custom-call(f32[4,128,256]{2,1,0:T(8,128)S(1)} %get-tuple-element.8.xs, f32[4,64,64]{2,1,0:T(8,128)S(1)} %copy-done, s32[1,256]{1,0:T(1,128)S(1)} %get-tuple-element.9.piv_in), custom_call_target="tpu_custom_call" | custom-call | tf_op jit(solution)/shard_map/factor/pallas_call | solution.py:477
Async XLA Ops:
  0.6 45.0 %copy-start = (f32[4,64,64]{2,1,0:T(8,128)S(1)}, f32[4,64,64]{2,1,0:T(8,128)}, u32[]{:S(2)}) copy-start(f32[4,64,64]{2,1,0:T(8,128)} %dinv.1) | copy-start | bytes 196612
